TPU v7x, 512 devices: a whole 4x8x8 slice. The times are simulated.
512 devices in a mesh: dp: 16 (over y, core), expert: 32 (over z, x).
Axes of the slice: x: 4, y: 8, z: 8, core: 2. Of those that a mesh axis runs over, the one named last changes fastest.
Arguments:
- stream_q: bfloat16 [4096, 4096], P('dp', 'expert'), may hold values from -6 to 6
- stream_k: bfloat16 [4096, 4096], P('dp', 'expert'), may hold values from -6 to 6
- stream_v: bfloat16 [4096, 4096], P('dp', 'expert'), may hold values from -6 to 6
- conv_taps: float32 [3, 3, 4096], P(None, None, 'expert'), may hold values from -14 to 14
- norm_gain: bfloat16 [4096], P('expert'), may hold values from 0.3984375 to 1.59375
- slot_token: int32 [16, 384], P('dp'), may hold values from 0 to 256, as said below
- expert_count: int32 [16, 2], P('dp'), may hold values from 0 to 256, as said below
- route_prob: float32 [4096], P('dp'), may hold values from 0.25 to 1
- w_proj: bfloat16 [4096, 2, 8192], P('dp', None, 'expert'), may hold values from -0.09375 to 0.09375
- grad_out: bfloat16 [4096, 8192], P('dp', 'expert'), may hold values from -0.75 to 0.75
Outputs:
- activation: bfloat16 [4096, 8192], P('dp', 'expert')
- weight_grad: float32 [4096, 2, 8192], P('dp', None, 'expert')
Inputs may be any that keep to these rules, and one draw needn't show every extreme that they name: `slot_token`: for each index of dp the slots hold its 256 local token numbers, each exactly once, grouped by expert in expert order; each group starts at a multiple of 128 and is padded with the value 256 up to a multiple of 128; all slots after the last group hold 256. `expert_count`: the size of each expert's group in slot_token, before padding; each row sums to 256.
All inputs are finite; a program needn't handle non-finite values.
Results may differ from a plain program's by a relative error of at most 0.023.
Values may be sent and summed in bfloat16 or wider, within the bound.
No kernel may reach another device: no remote copies, remote signals or barrier semaphores. Data moves between devices by JAX's collectives and lax.ppermute only.
A program may use at most 64 MiB of HBM per device.

v0:
```python
import jax
import jax.numpy as jnp
from jax import lax
from jax.sharding import PartitionSpec as P

D = 4096
BLOCK = 128
epsilon = 1e-06


def from_behind(value, axis, steps):
    count = lax.axis_size(axis)
    leading, last = (max(0, -steps), min(count, count - steps))
    return lax.ppermute(value, axis, [(source, source + steps) for source in range(leading, last)])


def block_owner(counts, num_blocks):
    padded = (counts + BLOCK - 1) // BLOCK * BLOCK
    ends = jnp.cumsum(padded)
    starts = jnp.arange(num_blocks, dtype=jnp.int32) * BLOCK
    owner = jnp.sum((starts[:, None] >= ends[None, :]).astype(jnp.int32), axis=1)
    return jnp.minimum(owner, counts.shape[0] - 1)


def on_device(
    stream_q,
    stream_k,
    stream_v,
    conv_taps,
    norm_gain,
    slot_token,
    expert_count,
    route_prob,
    w_proj,
    grad_out,
):
    stacked = jnp.stack([stream_q, stream_k, stream_v])
    before = from_behind(stacked[:, -2:, :], "dp", 1)
    extended = jnp.concatenate([before, stacked], axis=1).astype(jnp.float32)
    convolved = (
        conv_taps[:, 0, None, :] * extended[:, 2:]
        + conv_taps[:, 1, None, :] * extended[:, 1:-1]
        + conv_taps[:, 2, None, :] * extended[:, :-2]
    )
    mixed = (convolved[0] * convolved[1] * convolved[2]).astype(jnp.bfloat16)
    mixed_f = mixed.astype(jnp.float32)
    total = lax.psum(jnp.sum(mixed_f * mixed_f, axis=1), "expert")
    inv_rms = lax.rsqrt(total / D + epsilon)
    normed = (mixed_f * inv_rms[:, None] * norm_gain.astype(jnp.float32)).astype(jnp.bfloat16)
    gathered = lax.all_gather(normed, "expert", axis=1, tiled=True)
    tok_count = gathered.shape[0]
    slots = slot_token[0]
    num_blocks = slots.shape[0] // BLOCK
    owner = block_owner(expert_count[0], num_blocks)
    padded_rows = jnp.concatenate(
        [gathered, jnp.zeros((1, gathered.shape[1]), jnp.bfloat16)], axis=0
    )
    x_blocks = padded_rows[slots].reshape(num_blocks, BLOCK, gathered.shape[1])
    hid_local = w_proj.shape[2]
    experts_here = w_proj.shape[1]
    selector = (owner[:, None] == jnp.arange(experts_here, dtype=jnp.int32)[None, :]).astype(
        jnp.bfloat16
    )
    columns = x_blocks
    chosen_w = jnp.einsum(
        "neh,be->bnh",
        lax.all_gather(w_proj, "dp", axis=0, tiled=True),
        selector,
        preferred_element_type=jnp.float32,
    ).astype(jnp.bfloat16)
    pre_act = jnp.einsum("brn,bnh->brh", columns, chosen_w, preferred_element_type=jnp.float32)
    pre_act = pre_act.reshape(num_blocks * BLOCK, hid_local)
    slot_prob = jnp.concatenate([route_prob, jnp.zeros((1,), jnp.float32)])[slots][:, None]
    sigmoid_z = jax.nn.sigmoid(pre_act)
    hidden = (slot_prob * pre_act * sigmoid_z).astype(jnp.bfloat16)
    activation = (
        jnp.zeros((tok_count + 1, hid_local), jnp.bfloat16).at[slots].set(hidden)[:tok_count]
    )
    slot_grad = jnp.concatenate([grad_out, jnp.zeros((1, hid_local), jnp.bfloat16)], axis=0)[
        slots
    ].astype(jnp.float32)
    grad_pre = (slot_grad * slot_prob * sigmoid_z * (1.0 + pre_act * (1.0 - sigmoid_z))).astype(
        jnp.bfloat16
    )
    grad_blocks = grad_pre.reshape(num_blocks, BLOCK, hid_local)
    masked_grad = grad_blocks[None, :, :, :] * selector.T[:, :, None, None]
    columns = x_blocks
    weight_grad = lax.psum_scatter(
        jnp.einsum(
            "brd,ebrh->deh", columns, masked_grad, preferred_element_type=jnp.float32
        ).astype(jnp.bfloat16),
        "dp",
        scatter_dimension=0,
        tiled=True,
    ).astype(jnp.float32)
    return (activation, weight_grad)


def solution(mesh):
    placed = (
        P("dp", "expert"),
        P("dp", "expert"),
        P("dp", "expert"),
        P(None, None, "expert"),
        P("expert"),
        P("dp", None),
        P("dp", None),
        P("dp"),
        P("dp", None, "expert"),
        P("dp", "expert"),
    )
    return jax.shard_map(
        on_device,
        mesh=mesh,
        in_specs=placed,
        out_specs=(P("dp", "expert"), P("dp", None, "expert")),
        check_vma=False,
    )
```

profile of v0, /device:TPU:29, one launch (start us, length us, event | category | flops | bytes accessed | tf_op | source)
XLA Modules:
  0.0 303.6 jit_solution(1994741817525698117)
XLA Ops:
  7.2 0.0 copy-start.2
  7.2 0.0 copy-start.3
  7.2 0.0 all-gather.3.cloned.1.call-start
  7.2 0.7 pad_maximum_fusion.1
  8.0 5.0 %collective-permute-start = (bf16[3,2,128]{2,1,0:T(2,128)(2,1)S(1)}, bf16[3,2,128]{2,1,0:T(2,128)(2,1)S(1)}, u32[]{:S(2)}, u32[]{:S(2)}) collective-permute-start(bf16[3,2,128]{2,1,0:T(2,128)(2,1)S(1)} %pad_maximum_fusion.1), channel_id=1, source_target_pairs={{0,32},{32,64},{64,96},{96,128},{128,160},{160,192},{192,224},{224... | collective-permute-start | bytes 4616 | tf_op jit(solution)/shard_map/ppermute | solution.py:14
  12.9 0.8 fusion.29
  13.8 0.7 convert_element_type.59
  14.4 0.0 collective-permute-done
  14.4 0.9 maximum_convert_fusion
  15.4 0.1 fusion.2
  15.5 0.1 fusion.15
  15.6 62.6 %psum.7 = f32[256]{0:T(256)S(1)} all-reduce(f32[256]{0:T(256)S(1)} %get-tuple-element.10), channel_id=1, replica_groups=mesh['dp'=16,'expert'=32] {'expert'}, use_global_device_ids=true, to_apply=%region_1.0 | all-reduce | flops 256 | bytes 2048 | tf_op jit(solution)/shard_map/psum | solution.py:47
  78.2 0.7 fusion.17
  79.0 0.0 all-gather.3.cloned.1.call-update
  79.0 0.0 all-gather.5.cloned.1.call-start
  79.0 0.7 all-gather.5.cloned.1.call-update
  79.7 0.0 reduce-scatter.2.cloned.1.call-start
  79.8 0.7 pad_maximum_fusion
  80.5 0.7 fusion.24
  81.2 2.8 gather_fusion
  84.0 0.0 copy-done.2
  84.0 2.6 gather_fusion.2
  86.6 0.0 copy-done.3
  86.6 0.2 reduce-window.8
  86.8 0.1 fusion.25
  86.9 81.5 %all-gather.3.cloned.1.call-done = bf16[256,4096]{1,0:T(8,128)(2,1)} async-done(((bf16[256,128]{1,0:T(8,128)(2,1)}), bf16[256,4096]{1,0:T(8,128)(2,1)}) %all-gather.3.cloned.1.call-update) | async-done | bytes 2097168 | tf_op jit(solution)/shard_map/all_gather | solution.py:50
  168.4 1.8 concatenate.14
  170.1 4.1 %gather_fusion.1 = bf16[384,4096]{1,0:T(8,128)(2,1)} fusion(bf16[257,4096]{1,0:T(8,128)(2,1)S(1)} %concatenate.14, s32[1024]{0:T(1024)S(1)} %pad_clamp_fusion), kind=kCustom, calls=%fused_computation.1 | custom fusion | bytes 6292992 | tf_op jit(solution)/shard_map/gather | solution.py:58
  174.2 0.0 copy-start
  174.2 42.7 %all-gather.5.cloned.1.call-done = bf16[4096,2,256]{2,1,0:T(2,128)(2,1)} async-done(((bf16[256,2,256]{2,1,0:T(2,128)(2,1)}), bf16[4096,2,256]{2,1,0:T(2,128)(2,1)}) %all-gather.5.cloned.1.call-update) | async-done | bytes 4194320 | tf_op jit(solution)/shard_map/all_gather | solution.py:67
  217.0 0.0 copy-start.1
  217.0 7.5 %convolution_convert_fusion = bf16[3,4096,256]{2,0,1:T(4,128)(2,1)S(1)} fusion(bf16[4096,2,256]{2,1,0:T(2,128)(2,1)} %all-gather.5.cloned.1.call-done, s32[3]{0:T(128)S(1)} %broadcast_minimum_fusion), kind=kOutput, calls=%fused_computation.5 | convolution fusion | flops 15728646 | bytes 10485772 | tf_op jit(solution)/shard_map/neh,be->bnh/dot_general | solution.py:65
  224.4 0.0 copy-done
  224.5 0.0 copy-done.1
  224.5 1.3 fusion.6
  225.8 4.4 %bitcast_convert_fusion = bf16[4096,2,256]{2,0,1:T(8,128)(2,1)} fusion(bf16[3,128,4096,1]{2,1,0,3:T(8,128)(2,1)S(1)} %bitcast.50, bf16[2,3]{1,0:T(2,128)(2,1)S(1)} %compare_convert_fusion, bf16[3,128,256]{2,1,0:T(8,128)(2,1)S(1)} %get-tuple-element.15), kind=kOutput, calls=%fused_computation.4 | convolution fusion | flops 1613496320 | bytes 7536652 | tf_op jit(solution)/shard_map/brd,ebrh->deh/dot_general | solution.py:89
  230.1 0.0 reduce-scatter.2.cloned.1.call-update
  230.2 0.1 fusion.8
  230.3 1.9 scatter_custom_fusion
  232.2 0.7 slice.56
  232.8 62.2 %reduce-scatter.2.cloned.1.call-done = bf16[256,2,256]{2,0,1:T(8,128)(2,1)} async-done(((bf16[4096,2,256]{2,0,1:T(8,128)(2,1)}), bf16[256,2,256]{2,0,1:T(8,128)(2,1)}) %reduce-scatter.2.cloned.1.call-update) | async-done | bytes 262160 | tf_op jit(solution)/shard_map/reduce_scatter | solution.py:88
  295.1 2.0 copy.21
  (9 shorter events, 0.1 us)
Async XLA Ops:
  7.2 76.8 %copy-start.2 = (bf16[256,256]{1,0:T(8,128)(2,1)S(1)}, bf16[256,256]{1,0:T(8,128)(2,1)}, u32[]{:S(2)}) copy-start(bf16[256,256]{1,0:T(8,128)(2,1)} %param.19) | copy-start | bytes 393220
  7.2 79.4 %copy-start.3 = (s32[1,2]{1,0:T(1,128)S(1)}, s32[1,2]{1,0:T(1,128)}, u32[]{:S(2)}) copy-start(s32[1,2]{1,0:T(1,128)} %param.16) | copy-start | bytes 28
  7.2 161.2 %all-gather.3.cloned.1.call-start = ((), (), s32[]{:S(2)}) async-start(), calls=%async_computation.1 | async-start | bytes 2162688 | tf_op jit(solution)/shard_map/all_gather | solution.py:50
  8.0 6.5 %collective-permute-start = (bf16[3,2,128]{2,1,0:T(2,128)(2,1)S(1)}, bf16[3,2,128]{2,1,0:T(2,128)(2,1)S(1)}, u32[]{:S(2)}, u32[]{:S(2)}) collective-permute-start(bf16[3,2,128]{2,1,0:T(2,128)(2,1)S(1)} %pad_maximum_fusion.1), channel_id=1, source_target_pairs={{0,32},{32,64},{64,96},{96,128},{128,160},{160,192},{192,224},{224... | collective-permute-start | bytes 4616 | tf_op jit(solution)/shard_map/ppermute | solution.py:14
  79.0 138.0 %all-gather.5.cloned.1.call-start = ((), (), s32[]{:S(2)}) async-start(), calls=%async_computation.2 | async-start | bytes 4456448 | tf_op jit(solution)/shard_map/all_gather | solution.py:67
  79.7 215.3 %reduce-scatter.2.cloned.1.call-start = ((), (), s32[]{:S(2)}) async-start(), calls=%async_computation.3 | async-start | bytes 4456448 | tf_op jit(solution)/shard_map/reduce_scatter | solution.py:88
  174.2 50.2 %copy-start = (bf16[384,4096]{1,0:T(8,128)(2,1)S(1)}, bf16[384,4096]{1,0:T(8,128)(2,1)}, u32[]{:S(2)}) copy-start(bf16[384,4096]{1,0:T(8,128)(2,1)} %gather_fusion.1) | copy-start | bytes 9437188
  217.0 7.5 %copy-start.1 = (bf16[384,256]{1,0:T(8,128)(2,1)S(1)}, bf16[384,256]{1,0:T(8,128)(2,1)}, u32[]{:S(2)}) copy-start(bf16[384,256]{1,0:T(8,128)(2,1)} %gather_fusion.2) | copy-start | bytes 589828
Sparse Core Ops, SparseCore 0:
  79.1 89.2 all-gather.2
  170.5 46.4 all-gather.4
  230.3 64.7 reduce-scatter.1
where the time goes:
time: 304 us
  waiting for transfers between devices  187 us (62%)
  blocking collectives  62.6 us (21%)
  local copies, waits for them, and re-layouts  16.6 us (5%)
  between operations  13.9 us (5%)
  matrix products  13.1 us (4%)
  other arithmetic  5.15 us (2%)
  starting transfers between devices  5.08 us (2%)
    all_gather x1, waiting for transfers between devices, on_device(): gathered = lax.all_gather(normed, 'expert', axis=1, tiled=True)  81.5 us
    psum x1, blocking collectives, on_device(): total = lax.psum(jnp.sum(mixed_f * mixed_f, axis=1), 'expert')  62.6 us
    reduce_scatter x1, waiting for transfers between devices, on_device(): lax.psum_scatter(jnp.einsum('brd,ebrh->deh', columns, masked_grad, prefer...  62.2 us
    all_gather x1, waiting for transfers between devices, on_device(): lax.all_gather(w_proj, 'dp', axis=0, tiled=True)  42.7 us
    dot_general x1, matrix products, on_device(): jnp.einsum('neh,be->bnh', lax.all_gather(w_proj, 'dp', axis=0, tiled=True...  7.48 us
  transfers between devices with their start and end apart: 4, of which 3 were waited for; matrix products, arithmetic and copies ran while one was open for 6% of the time, Pallas kernels for 0%

commit v1 on v0

--- a/solution.py
+++ b/solution.py
@@ -6,6 +6,20 @@
 D = 4096
 BLOCK = 128
 epsilon = 1e-06
+
+
+def work_both_ways(x, axis, dim, make, out_dim):
+    ways, here, hop = (lax.axis_size(axis), lax.axis_index(axis), x.shape[dim])
+    earlier, later = ([], [])
+    going_up = going_down = x
+    for far in range(ways // 2 + 1):
+        earlier.append(make(going_up, (here - far) % ways * hop))
+        if 0 < far < ways - ways // 2:
+            later.append(make(going_down, (here + far) % ways * hop))
+        going_up = lax.ppermute(going_up, axis, [(d, (d + 1) % ways) for d in range(ways)])
+        going_down = lax.ppermute(going_down, axis, [(d, (d - 1) % ways) for d in range(ways)])
+    line = jnp.concatenate([*earlier[::-1], *later], axis=out_dim)
+    return jnp.roll(line, (here - ways // 2) * earlier[0].shape[out_dim], axis=out_dim)
 
 
 def from_behind(value, axis, steps):
@@ -62,11 +76,14 @@
         jnp.bfloat16
     )
     columns = x_blocks
-    chosen_w = jnp.einsum(
-        "neh,be->bnh",
-        lax.all_gather(w_proj, "dp", axis=0, tiled=True),
-        selector,
-        preferred_element_type=jnp.float32,
+    chosen_w = work_both_ways(
+        w_proj,
+        "dp",
+        0,
+        lambda shard, offset: jnp.einsum(
+            "neh,be->bnh", shard, selector, preferred_element_type=jnp.float32
+        ),
+        1,
     ).astype(jnp.bfloat16)
     pre_act = jnp.einsum("brn,bnh->brh", columns, chosen_w, preferred_element_type=jnp.float32)
     pre_act = pre_act.reshape(num_blocks * BLOCK, hid_local)

time: 304 us -> 272 us (0.89)
  the two profiles are of different devices: /device:TPU:29 before, /device:TPU:25 now
where the time goes in v1:
time: 272 us
  waiting for transfers between devices  77.2 us (28%)
  blocking collectives  66.9 us (25%)
  starting transfers between devices  44.4 us (16%)
  local copies, waits for them, and re-layouts  43.1 us (16%)
  matrix products  20.3 us (7%)
  between operations  14.4 us (5%)
  other arithmetic  5.79 us (2%)
    psum x1, blocking collectives, on_device(): total = lax.psum(jnp.sum(mixed_f * mixed_f, axis=1), 'expert')  66.9 us
    reduce_scatter x1, waiting for transfers between devices, on_device(): lax.psum_scatter(jnp.einsum('brd,ebrh->deh', columns, masked_grad, prefer...  61.3 us
    ppermute x8, starting transfers between devices, work_both_ways(): lax.ppermute(going_up, axis, [(d, (d + 1) % ways) for d in range(ways)])  39.2 us
    unnamed x34, local copies, waits for them, and re-layouts  27.1 us
    ppermute x8, waiting for transfers between devices, work_both_ways(): lax.ppermute(going_up, axis, [(d, (d + 1) % ways) for d in range(ways)])  15.3 us
    dot_general x16, matrix products, on_device(): jnp.einsum('neh,be->bnh', shard, selector, preferred_element_type=jnp.flo...  9.22 us
    dot_general x1, matrix products, on_device(): jnp.einsum('brd,ebrh->deh', columns, masked_grad, preferred_element_type=...  6.29 us
  transfers between devices with their start and end apart: 18, of which 11 were waited for; matrix products, arithmetic and copies ran while one was open for 18% of the time, Pallas kernels for 0%

profile of v1, /device:TPU:25, one launch (start us, length us, event | category | flops | bytes accessed | tf_op | source)
XLA Modules:
  0.0 272.0 jit_solution(12949090356885046290)
XLA Ops:
  7.2 3.1 %collective-permute-start.1 = (bf16[256,2,256]{2,1,0:T(2,128)(2,1)}, bf16[256,2,256]{2,1,0:T(2,128)(2,1)S(1)}, u32[]{:S(2)}, u32[]{:S(2)}) collective-permute-start(bf16[256,2,256]{2,1,0:T(2,128)(2,1)} %param.18), channel_id=1, source_target_pairs={{0,32},{32,64},{64,96},{96,128},{128,160},{160,192},{192,224},{224... | collective-permute-start | bytes 786440 | tf_op jit(solution)/shard_map/ppermute | solution.py:19
  10.3 0.7 pad_maximum_fusion.1
  11.0 4.8 %collective-permute-start = (bf16[3,2,128]{2,1,0:T(2,128)(2,1)S(1)}, bf16[3,2,128]{2,1,0:T(2,128)(2,1)S(1)}, u32[]{:S(2)}, u32[]{:S(2)}) collective-permute-start(bf16[3,2,128]{2,1,0:T(2,128)(2,1)S(1)} %pad_maximum_fusion.1), channel_id=1, source_target_pairs={{0,32},{32,64},{64,96},{96,128},{128,160},{160,192},{192,224},{224... | collective-permute-start | bytes 4616 | tf_op jit(solution)/shard_map/ppermute | solution.py:28
  16.8 1.5 fusion.35
  18.3 0.8 fusion.73
  21.2 2.8 %gather_fusion = f32[384]{0:T(512)S(1)} fusion(f32[257]{0:T(512)S(1)} %pad_maximum_fusion, s32[1024]{0:T(1024)S(1)} %pad_clamp_fusion), kind=kCustom, calls=%fused_computation | custom fusion | bytes 4608 | tf_op jit(solution)/shard_map/gather | solution.py:90
  24.0 0.9 concatenate.22
  24.9 2.1 gather_fusion.2
  27.0 0.9 maximum_convert_fusion
  28.2 66.9 %psum.7 = f32[256]{0:T(256)S(1)} all-reduce(f32[256]{0:T(256)S(1)} %get-tuple-element.10), channel_id=1, replica_groups=mesh['dp'=16,'expert'=32] {'expert'}, use_global_device_ids=true, to_apply=%region_1.0 | all-reduce | flops 256 | bytes 2048 | tf_op jit(solution)/shard_map/psum | solution.py:61
  95.1 0.7 fusion.16
  96.1 14.0 %collective-permute-start.2 = (bf16[256,2,256]{2,1,0:T(2,128)(2,1)S(1)}, bf16[256,2,256]{2,1,0:T(2,128)(2,1)S(1)}, u32[]{:S(2)}, u32[]{:S(2)}) collective-permute-start(bf16[256,2,256]{2,1,0:T(2,128)(2,1)S(1)} %collective-permute-done.1), channel_id=1, source_target_pairs={{0,32},{32,64},{64,96},{96,128},{128,160},{160,192},{192,224},{224... | collective-permute-start | bytes 786440 | tf_op jit(solution)/shard_map/ppermute | solution.py:19
  111.2 2.2 collective-permute-done.2
  113.4 3.7 %collective-permute-start.3 = (bf16[256,2,256]{2,1,0:T(2,128)(2,1)S(1)}, bf16[256,2,256]{2,1,0:T(2,128)(2,1)S(1)}, u32[]{:S(2)}, u32[]{:S(2)}) collective-permute-start(bf16[256,2,256]{2,1,0:T(2,128)(2,1)S(1)} %collective-permute-done.2), channel_id=1, source_target_pairs={{0,32},{32,64},{64,96},{96,128},{128,160},{160,192},{192,224},{224... | collective-permute-start | bytes 786440 | tf_op jit(solution)/shard_map/ppermute | solution.py:19
  118.2 2.2 collective-permute-done.3
  120.4 3.7 %collective-permute-start.4 = (bf16[256,2,256]{2,1,0:T(2,128)(2,1)S(1)}, bf16[256,2,256]{2,1,0:T(2,128)(2,1)S(1)}, u32[]{:S(2)}, u32[]{:S(2)}) collective-permute-start(bf16[256,2,256]{2,1,0:T(2,128)(2,1)S(1)} %collective-permute-done.3), channel_id=1, source_target_pairs={{0,32},{32,64},{64,96},{96,128},{128,160},{160,192},{192,224},{224... | collective-permute-start | bytes 786440 | tf_op jit(solution)/shard_map/ppermute | solution.py:19
  125.2 2.2 collective-permute-done.4
  127.4 3.7 %collective-permute-start.5 = (bf16[256,2,256]{2,1,0:T(2,128)(2,1)S(1)}, bf16[256,2,256]{2,1,0:T(2,128)(2,1)S(1)}, u32[]{:S(2)}, u32[]{:S(2)}) collective-permute-start(bf16[256,2,256]{2,1,0:T(2,128)(2,1)S(1)} %collective-permute-done.4), channel_id=1, source_target_pairs={{0,32},{32,64},{64,96},{96,128},{128,160},{160,192},{192,224},{224... | collective-permute-start | bytes 786440 | tf_op jit(solution)/shard_map/ppermute | solution.py:19
  132.2 2.2 collective-permute-done.5
  134.4 3.7 %collective-permute-start.6 = (bf16[256,2,256]{2,1,0:T(2,128)(2,1)S(1)}, bf16[256,2,256]{2,1,0:T(2,128)(2,1)S(1)}, u32[]{:S(2)}, u32[]{:S(2)}) collective-permute-start(bf16[256,2,256]{2,1,0:T(2,128)(2,1)S(1)} %collective-permute-done.5), channel_id=1, source_target_pairs={{0,32},{32,64},{64,96},{96,128},{128,160},{160,192},{192,224},{224... | collective-permute-start | bytes 786440 | tf_op jit(solution)/shard_map/ppermute | solution.py:19
  139.3 2.1 collective-permute-done.6
  141.4 3.7 %collective-permute-start.7 = (bf16[256,2,256]{2,1,0:T(2,128)(2,1)S(1)}, bf16[256,2,256]{2,1,0:T(2,128)(2,1)S(1)}, u32[]{:S(2)}, u32[]{:S(2)}) collective-permute-start(bf16[256,2,256]{2,1,0:T(2,128)(2,1)S(1)} %collective-permute-done.6), channel_id=1, source_target_pairs={{0,32},{32,64},{64,96},{96,128},{128,160},{160,192},{192,224},{224... | collective-permute-start | bytes 786440 | tf_op jit(solution)/shard_map/ppermute | solution.py:19
  146.3 2.1 collective-permute-done.7
  148.4 3.7 %collective-permute-start.8 = (bf16[256,2,256]{2,1,0:T(2,128)(2,1)S(1)}, bf16[256,2,256]{2,1,0:T(2,128)(2,1)S(1)}, u32[]{:S(2)}, u32[]{:S(2)}) collective-permute-start(bf16[256,2,256]{2,1,0:T(2,128)(2,1)S(1)} %collective-permute-done.7), channel_id=1, source_target_pairs={{0,32},{32,64},{64,96},{96,128},{128,160},{160,192},{192,224},{224... | collective-permute-start | bytes 786440 | tf_op jit(solution)/shard_map/ppermute | solution.py:19
  153.3 2.1 collective-permute-done.8
  156.0 0.8 copy_dynamic-update-slice_fusion.30
  156.8 0.8 copy_dynamic-update-slice_fusion.28
  157.6 0.8 copy_dynamic-update-slice_fusion.26
  158.4 0.8 copy_dynamic-update-slice_fusion.24
  159.2 0.8 copy_dynamic-update-slice_fusion.22
  160.0 0.8 copy_dynamic-update-slice_fusion.20
  160.9 0.8 copy_dynamic-update-slice_fusion.18
  161.7 0.8 copy_dynamic-update-slice_fusion.16
  162.5 0.8 copy_dynamic-update-slice_fusion.14
  163.3 0.8 copy_dynamic-update-slice_fusion.12
  164.1 0.8 copy_dynamic-update-slice_fusion.10
  164.9 0.8 copy_dynamic-update-slice_fusion.8
  165.7 0.8 copy_dynamic-update-slice_fusion.6
  166.6 0.8 copy_dynamic-update-slice_fusion.4
  167.4 0.8 copy_dynamic-update-slice_fusion.2
  168.2 0.8 copy_dynamic-update-slice_fusion
  169.0 0.8 copy_dynamic-update-slice_fusion.31
  169.8 0.8 copy_dynamic-update-slice_fusion.29
  170.6 0.8 copy_dynamic-update-slice_fusion.27
  171.4 0.8 copy_dynamic-update-slice_fusion.25
  172.2 0.8 copy_dynamic-update-slice_fusion.23
  173.0 0.8 copy_dynamic-update-slice_fusion.21
  173.8 0.8 copy_dynamic-update-slice_fusion.19
  174.6 0.8 copy_dynamic-update-slice_fusion.17
  175.4 0.8 copy_dynamic-update-slice_fusion.15
  176.2 0.8 copy_dynamic-update-slice_fusion.13
  177.0 0.8 copy_dynamic-update-slice_fusion.11
  177.8 0.8 copy_dynamic-update-slice_fusion.9
  178.6 0.8 copy_dynamic-update-slice_fusion.7
  179.4 0.8 copy_dynamic-update-slice_fusion.5
  180.2 0.8 copy_dynamic-update-slice_fusion.3
  181.1 0.8 copy_dynamic-update-slice_fusion.1
  181.9 1.8 concatenate.20
  183.7 4.3 %gather_fusion.1 = bf16[384,4096]{1,0:T(8,128)(2,1)} fusion(bf16[257,4096]{1,0:T(8,128)(2,1)S(1)} %concatenate.20, s32[1024]{0:T(1024)S(1)} %pad_clamp_fusion), kind=kCustom, calls=%fused_computation.1 | custom fusion | bytes 6292992 | tf_op jit(solution)/shard_map/gather | solution.py:72
  187.9 4.8 %fusion.5 = (bf16[3,128,256]{2,1,0:T(8,128)(2,1)S(1)}, f32[3,128,256]{2,1,0:T(8,128)S(1)}) fusion(bf16[3,128,256]{2,1,0:T(8,128)(2,1)S(1)} %bitcast.102, f32[3,128]{1,0:T(4,128)S(1)} %bitcast.104, bf16[3,128,4096]{2,1,0:T(8,128)(2,1)} %bitcast.94, bf16[3,8192,256]{2,1,0:T(8,128)(2,1)} %copy_dynamic-update-slice_fusion.1, s32[]{:T(128)S(6)} %select_n.38), kind=kOutput, calls=%fused_computation.47 | convolution fusion | flops 806387712 | bytes 10225156 | tf_op jit(solution)/shard_map/brn,bnh->brh/dot_general | solution.py:88
  192.8 6.3 %bitcast_convert_fusion = bf16[4096,2,256]{2,0,1:T(8,128)(2,1)} fusion(bf16[3,128,4096,1]{2,1,0,3:T(8,128)(2,1)} %bitcast.95, bf16[2,3]{1,0:T(2,128)(2,1)S(1)} %compare_convert_fusion, bf16[3,128,256]{2,1,0:T(8,128)(2,1)S(1)} %get-tuple-element.15), kind=kOutput, calls=%fused_computation.5 | convolution fusion | flops 1613496320 | bytes 7536652 | tf_op jit(solution)/shard_map/brd,ebrh->deh/dot_general | solution.py:106
  199.2 1.9 scatter_custom_fusion
  201.8 61.3 %reduce-scatter.2.cloned.1.call-done = bf16[256,2,256]{2,0,1:T(8,128)(2,1)} async-done(((bf16[4096,2,256]{2,0,1:T(8,128)(2,1)}), bf16[256,2,256]{2,0,1:T(8,128)(2,1)}) %reduce-scatter.2.cloned.1.call-update) | async-done | bytes 262160 | tf_op jit(solution)/shard_map/reduce_scatter | solution.py:105
  263.1 2.0 copy.52
  (53 shorter events, 12.6 us)
Async XLA Ops:
  7.2 174.7 %all-gather.2.cloned.1.call-start = ((), (), s32[]{:S(2)}) async-start(), calls=%async_computation.1 | async-start | bytes 2162688 | tf_op jit(solution)/shard_map/all_gather | solution.py:64
  7.2 88.9 %collective-permute-start.1 = (bf16[256,2,256]{2,1,0:T(2,128)(2,1)}, bf16[256,2,256]{2,1,0:T(2,128)(2,1)S(1)}, u32[]{:S(2)}, u32[]{:S(2)}) collective-permute-start(bf16[256,2,256]{2,1,0:T(2,128)(2,1)} %param.18), channel_id=1, source_target_pairs={{0,32},{32,64},{64,96},{96,128},{128,160},{160,192},{192,224},{224... | collective-permute-start | bytes 786440 | tf_op jit(solution)/shard_map/ppermute | solution.py:19
  10.3 100.3 %collective-permute-start.9 = (bf16[256,2,256]{2,1,0:T(2,128)(2,1)}, bf16[256,2,256]{2,1,0:T(2,128)(2,1)S(1)}, u32[]{:S(2)}, u32[]{:S(2)}) collective-permute-start(bf16[256,2,256]{2,1,0:T(2,128)(2,1)} %param.18), channel_id=1, source_target_pairs={{0,480},{32,0},{64,32},{96,64},{128,96},{160,128},{192,160},{224,1... | collective-permute-start | bytes 786440 | tf_op jit(solution)/shard_map/ppermute | solution.py:20
  11.0 16.0 %collective-permute-start = (bf16[3,2,128]{2,1,0:T(2,128)(2,1)S(1)}, bf16[3,2,128]{2,1,0:T(2,128)(2,1)S(1)}, u32[]{:S(2)}, u32[]{:S(2)}) collective-permute-start(bf16[3,2,128]{2,1,0:T(2,128)(2,1)S(1)} %pad_maximum_fusion.1), channel_id=1, source_target_pairs={{0,32},{32,64},{64,96},{96,128},{128,160},{160,192},{192,224},{224... | collective-permute-start | bytes 4616 | tf_op jit(solution)/shard_map/ppermute | solution.py:28
  95.9 167.3 %reduce-scatter.2.cloned.1.call-start = ((), (), s32[]{:S(2)}) async-start(), calls=%async_computation.2 | async-start | bytes 4456448 | tf_op jit(solution)/shard_map/reduce_scatter | solution.py:105
  96.1 17.3 %collective-permute-start.2 = (bf16[256,2,256]{2,1,0:T(2,128)(2,1)S(1)}, bf16[256,2,256]{2,1,0:T(2,128)(2,1)S(1)}, u32[]{:S(2)}, u32[]{:S(2)}) collective-permute-start(bf16[256,2,256]{2,1,0:T(2,128)(2,1)S(1)} %collective-permute-done.1), channel_id=1, source_target_pairs={{0,32},{32,64},{64,96},{96,128},{128,160},{160,192},{192,224},{224... | collective-permute-start | bytes 786440 | tf_op jit(solution)/shard_map/ppermute | solution.py:19
  110.6 7.0 %collective-permute-start.10 = (bf16[256,2,256]{2,1,0:T(2,128)(2,1)S(1)}, bf16[256,2,256]{2,1,0:T(2,128)(2,1)S(1)}, u32[]{:S(2)}, u32[]{:S(2)}) collective-permute-start(bf16[256,2,256]{2,1,0:T(2,128)(2,1)S(1)} %collective-permute-done.9), channel_id=1, source_target_pairs={{0,480},{32,0},{64,32},{96,64},{128,96},{160,128},{192,160},{224,1... | collective-permute-start | bytes 786440 | tf_op jit(solution)/shard_map/ppermute | solution.py:20
  113.4 7.0 %collective-permute-start.3 = (bf16[256,2,256]{2,1,0:T(2,128)(2,1)S(1)}, bf16[256,2,256]{2,1,0:T(2,128)(2,1)S(1)}, u32[]{:S(2)}, u32[]{:S(2)}) collective-permute-start(bf16[256,2,256]{2,1,0:T(2,128)(2,1)S(1)} %collective-permute-done.2), channel_id=1, source_target_pairs={{0,32},{32,64},{64,96},{96,128},{128,160},{160,192},{192,224},{224... | collective-permute-start | bytes 786440 | tf_op jit(solution)/shard_map/ppermute | solution.py:19
  117.6 7.0 %collective-permute-start.11 = (bf16[256,2,256]{2,1,0:T(2,128)(2,1)S(1)}, bf16[256,2,256]{2,1,0:T(2,128)(2,1)S(1)}, u32[]{:S(2)}, u32[]{:S(2)}) collective-permute-start(bf16[256,2,256]{2,1,0:T(2,128)(2,1)S(1)} %collective-permute-done.10), channel_id=1, source_target_pairs={{0,480},{32,0},{64,32},{96,64},{128,96},{160,128},{192,160},{224,1... | collective-permute-start | bytes 786440 | tf_op jit(solution)/shard_map/ppermute | solution.py:20
  120.4 7.0 %collective-permute-start.4 = (bf16[256,2,256]{2,1,0:T(2,128)(2,1)S(1)}, bf16[256,2,256]{2,1,0:T(2,128)(2,1)S(1)}, u32[]{:S(2)}, u32[]{:S(2)}) collective-permute-start(bf16[256,2,256]{2,1,0:T(2,128)(2,1)S(1)} %collective-permute-done.3), channel_id=1, source_target_pairs={{0,32},{32,64},{64,96},{96,128},{128,160},{160,192},{192,224},{224... | collective-permute-start | bytes 786440 | tf_op jit(solution)/shard_map/ppermute | solution.py:19
  124.7 7.0 %collective-permute-start.12 = (bf16[256,2,256]{2,1,0:T(2,128)(2,1)S(1)}, bf16[256,2,256]{2,1,0:T(2,128)(2,1)S(1)}, u32[]{:S(2)}, u32[]{:S(2)}) collective-permute-start(bf16[256,2,256]{2,1,0:T(2,128)(2,1)S(1)} %collective-permute-done.11), channel_id=1, source_target_pairs={{0,480},{32,0},{64,32},{96,64},{128,96},{160,128},{192,160},{224,1... | collective-permute-start | bytes 786440 | tf_op jit(solution)/shard_map/ppermute | solution.py:20
  127.4 7.0 %collective-permute-start.5 = (bf16[256,2,256]{2,1,0:T(2,128)(2,1)S(1)}, bf16[256,2,256]{2,1,0:T(2,128)(2,1)S(1)}, u32[]{:S(2)}, u32[]{:S(2)}) collective-permute-start(bf16[256,2,256]{2,1,0:T(2,128)(2,1)S(1)} %collective-permute-done.4), channel_id=1, source_target_pairs={{0,32},{32,64},{64,96},{96,128},{128,160},{160,192},{192,224},{224... | collective-permute-start | bytes 786440 | tf_op jit(solution)/shard_map/ppermute | solution.py:19
  131.7 7.1 %collective-permute-start.13 = (bf16[256,2,256]{2,1,0:T(2,128)(2,1)S(1)}, bf16[256,2,256]{2,1,0:T(2,128)(2,1)S(1)}, u32[]{:S(2)}, u32[]{:S(2)}) collective-permute-start(bf16[256,2,256]{2,1,0:T(2,128)(2,1)S(1)} %collective-permute-done.12), channel_id=1, source_target_pairs={{0,480},{32,0},{64,32},{96,64},{128,96},{160,128},{192,160},{224,1... | collective-permute-start | bytes 786440 | tf_op jit(solution)/shard_map/ppermute | solution.py:20
  134.4 7.0 %collective-permute-start.6 = (bf16[256,2,256]{2,1,0:T(2,128)(2,1)S(1)}, bf16[256,2,256]{2,1,0:T(2,128)(2,1)S(1)}, u32[]{:S(2)}, u32[]{:S(2)}) collective-permute-start(bf16[256,2,256]{2,1,0:T(2,128)(2,1)S(1)} %collective-permute-done.5), channel_id=1, source_target_pairs={{0,32},{32,64},{64,96},{96,128},{128,160},{160,192},{192,224},{224... | collective-permute-start | bytes 786440 | tf_op jit(solution)/shard_map/ppermute | solution.py:19
  138.8 7.0 %collective-permute-start.14 = (bf16[256,2,256]{2,1,0:T(2,128)(2,1)S(1)}, bf16[256,2,256]{2,1,0:T(2,128)(2,1)S(1)}, u32[]{:S(2)}, u32[]{:S(2)}) collective-permute-start(bf16[256,2,256]{2,1,0:T(2,128)(2,1)S(1)} %collective-permute-done.13), channel_id=1, source_target_pairs={{0,480},{32,0},{64,32},{96,64},{128,96},{160,128},{192,160},{224,1... | collective-permute-start | bytes 786440 | tf_op jit(solution)/shard_map/ppermute | solution.py:20
  141.4 7.0 %collective-permute-start.7 = (bf16[256,2,256]{2,1,0:T(2,128)(2,1)S(1)}, bf16[256,2,256]{2,1,0:T(2,128)(2,1)S(1)}, u32[]{:S(2)}, u32[]{:S(2)}) collective-permute-start(bf16[256,2,256]{2,1,0:T(2,128)(2,1)S(1)} %collective-permute-done.6), channel_id=1, source_target_pairs={{0,32},{32,64},{64,96},{96,128},{128,160},{160,192},{192,224},{224... | collective-permute-start | bytes 786440 | tf_op jit(solution)/shard_map/ppermute | solution.py:19
  145.8 7.0 %collective-permute-start.15 = (bf16[256,2,256]{2,1,0:T(2,128)(2,1)S(1)}, bf16[256,2,256]{2,1,0:T(2,128)(2,1)S(1)}, u32[]{:S(2)}, u32[]{:S(2)}) collective-permute-start(bf16[256,2,256]{2,1,0:T(2,128)(2,1)S(1)} %collective-permute-done.14), channel_id=1, source_target_pairs={{0,480},{32,0},{64,32},{96,64},{128,96},{160,128},{192,160},{224,1... | collective-permute-start | bytes 786440 | tf_op jit(solution)/shard_map/ppermute | solution.py:20
  148.4 7.0 %collective-permute-start.8 = (bf16[256,2,256]{2,1,0:T(2,128)(2,1)S(1)}, bf16[256,2,256]{2,1,0:T(2,128)(2,1)S(1)}, u32[]{:S(2)}, u32[]{:S(2)}) collective-permute-start(bf16[256,2,256]{2,1,0:T(2,128)(2,1)S(1)} %collective-permute-done.7), channel_id=1, source_target_pairs={{0,32},{32,64},{64,96},{96,128},{128,160},{160,192},{192,224},{224... | collective-permute-start | bytes 786440 | tf_op jit(solution)/shard_map/ppermute | solution.py:19
Sparse Core Ops, SparseCore 0:
  96.0 82.1 all-gather.1
  199.2 63.8 reduce-scatter.1
